TPU v7x, 256 devices: a whole 4x4x8 slice. The times are simulated.
256 devices in a mesh: band: 64 (over x, y_hi, z), grid: 4 (over y_lo, core).
Axes of the slice: x: 4, y: 4 (y_hi: 2, y_lo: 2; y = y_hi * 2 + y_lo), z: 8, core: 2. Of those that a mesh axis runs over, the one named last changes fastest.
Arguments:
- bands: float32 [128, 96, 96, 96], P('band', 'grid'), may hold values from -6 to 6
Outputs:
- exchange_out: float32 [128, 96, 96, 96], P('band', 'grid')
All inputs are finite; a program needn't handle non-finite values.
Results may differ from a plain program's by a relative error of at most 0.0091.
Values may be sent and summed in bfloat16 or wider, within the bound.
No kernel may reach another device: no remote copies, remote signals or barrier semaphores. Data moves between devices by JAX's collectives and lax.ppermute only.
A program may use at most 128 MiB of HBM per device.

v0:
```python
import jax
import jax.numpy as jnp
import numpy as np
from jax import lax
from jax.sharding import PartitionSpec as P

ROUNDS = 3


kernel_scale = 16.0
screen_sq = 0.05


def passed_along(value, axis, by):
    length = lax.axis_size(axis)
    return lax.ppermute(value, axis, [(i, (i + by) % length) for i in range(length)])


def dft_table(length):
    half = length // 2
    rows = np.arange(length)
    freq = np.where(rows <= half, rows, rows - half)
    phase = 2.0 * np.pi * np.outer(freq, rows) / length
    return np.where((rows <= half)[:, None], np.cos(phase), np.sin(phase))


def frequency_weights(rows, length):
    half = length // 2
    freq = jnp.where(rows <= half, rows, rows - half).astype(jnp.float32)
    weight = jnp.where((rows == 0) | (rows == half), 1.0, 2.0).astype(jnp.float32) / length
    return (freq, weight)


def multiplier(rows_x, rows_y, rows_z, length):
    freq_x, weight_x = frequency_weights(rows_x, length)
    freq_y, weight_y = frequency_weights(rows_y, length)
    freq_z, weight_z = frequency_weights(rows_z, length)
    square = freq_x[:, None, None] ** 2 + freq_y[None, :, None] ** 2 + freq_z[None, None, :] ** 2
    scale = weight_x[:, None, None] * weight_y[None, :, None] * weight_z[None, None, :]
    return kernel_scale * scale / (square + screen_sq)


def apply_table(form, cosines, data):
    return jnp.einsum(form, cosines, data, preferred_element_type=jnp.float32)


def forward_local(density, cosines):
    section_one = apply_table("cz,pxyz->pxyc", cosines, density).astype(jnp.bfloat16)
    return apply_table("cy,pxyz->pxcz", cosines, section_one).astype(jnp.bfloat16)


def first_axis(section_two, cosines, weights):
    section_three = (weights[None] * apply_table("cx,pxyz->pcyz", cosines, section_two)).astype(
        jnp.bfloat16
    )
    return apply_table("cx,pcyz->pxyz", cosines, section_three).astype(jnp.bfloat16)


def inverse_local(section_four, cosines):
    section_five = apply_table("cy,pxcz->pxyz", cosines, section_four).astype(jnp.bfloat16)
    return apply_table("cz,pxyc->pxyz", cosines, section_five).astype(jnp.bfloat16)


def per_device(bands):
    own_copies = bands.astype(jnp.bfloat16)
    band_count = own_copies.shape[0]
    planes = own_copies.shape[1]
    length = own_copies.shape[2]
    grid_count = lax.axis_size("grid")
    cosines = jnp.asarray(dft_table(length), jnp.bfloat16)
    indices = jnp.arange(length, dtype=jnp.int32)
    partners = []
    current = passed_along(own_copies, "band", 1)
    partners.append(current)
    for round_index in range(2, ROUNDS + 1):
        current = passed_along(current, "band", 1)
        partners.append(current)
    summed = jnp.zeros(own_copies.shape, jnp.float32)
    for round_index in range(1, ROUNDS + 1):
        partner = partners[round_index - 1]
        density = (
            own_copies[:, None].astype(jnp.float32) * partner[None].astype(jnp.float32)
        ).astype(jnp.bfloat16)
        density = density.reshape(band_count * band_count, planes, length, length)
        grouped = density.reshape(
            grid_count, band_count * band_count // grid_count, planes, length, length
        )
        full_weights = multiplier(indices, indices, indices, length)
        spectra = lax.all_to_all(grouped, "grid", split_axis=0, concat_axis=2, tiled=True)
        flat = spectra.reshape(spectra.shape[1], length, length, length)
        section_two = forward_local(flat, cosines)
        section_four = first_axis(section_two, cosines, full_weights)
        potential = inverse_local(section_four, cosines).reshape(spectra.shape)
        potential = lax.all_to_all(potential, "grid", split_axis=2, concat_axis=0, tiled=True)
        potential = potential.reshape(band_count * band_count, planes, length, length)
        field = potential.reshape(band_count, band_count, planes, length, length)
        own_terms = jnp.einsum(
            "ijxyz,jxyz->ixyz", field, partner, preferred_element_type=jnp.float32
        )
        given = jnp.einsum(
            "ijxyz,ixyz->jxyz", field, own_copies, preferred_element_type=jnp.float32
        ).astype(jnp.bfloat16)
        returned = passed_along(given, "band", -round_index)
        summed = summed + own_terms + returned.astype(jnp.float32)
    return -summed


def solution(mesh):
    in_specs = (P("band", "grid", None, None),)
    out_specs = P("band", "grid", None, None)
    return jax.shard_map(
        per_device, mesh=mesh, in_specs=in_specs, out_specs=out_specs, check_vma=False
    )
```

profile of v0, /device:TPU:32, one launch (start us, length us, event | category | flops | bytes accessed | tf_op | source)
XLA Modules:
  0.0 466.9 jit_solution(2401626935075811122)
XLA Ops:
  0.0 3.5 bitcast_convert_fusion.2
  5.4 25.8 %collective-permute-done = bf16[2,24,96,96]{3,2,1,0:T(8,128)(2,1)S(1)} collective-permute-done((bf16[2,24,96,96]{3,2,1,0:T(8,128)(2,1)S(1)}, bf16[2,24,96,96]{3,2,1,0:T(8,128)(2,1)S(1)}, u32[]{:S(2)}, u32[]{:S(2)}) %collective-permute-start) | collective-permute-done | bytes 884768 | tf_op jit(solution)/shard_map/ppermute | solution.py:16
  33.1 32.5 %collective-permute-done.2 = bf16[2,24,96,96]{3,2,1,0:T(8,128)(2,1)S(1)} collective-permute-done((bf16[2,24,96,96]{3,2,1,0:T(8,128)(2,1)S(1)}, bf16[2,24,96,96]{3,2,1,0:T(8,128)(2,1)S(1)}, u32[]{:S(2)}, u32[]{:S(2)}) %collective-permute-start.2) | collective-permute-done | bytes 884768 | tf_op jit(solution)/shard_map/ppermute | solution.py:16
  69.4 28.2 %collective-permute-done.4 = bf16[2,24,96,96]{3,2,1,0:T(8,128)(2,1)S(1)} collective-permute-done((bf16[2,24,96,96]{3,2,1,0:T(8,128)(2,1)S(1)}, bf16[2,24,96,96]{3,2,1,0:T(8,128)(2,1)S(1)}, u32[]{:S(2)}, u32[]{:S(2)}) %collective-permute-start.4) | collective-permute-done | bytes 884768 | tf_op jit(solution)/shard_map/ppermute | solution.py:16
  102.2 31.8 %all_to_all.24 = bf16[4,1,24,96,96]{4,3,2,1,0:T(8,128)(2,1)} all-to-all(bf16[4,1,24,96,96]{4,3,2,1,0:T(8,128)(2,1)S(1)} %bitcast.216), channel_id=1, replica_groups=mesh['band'=64,'grid'=4] {'grid'}, dimensions={0} | all-to-all | bytes 3538944 | tf_op jit(solution)/shard_map/all_to_all | solution.py:89
  133.9 3.6 all-to-all-start.2
  137.7 28.4 %all-to-all-done.2 = bf16[4,1,24,96,96]{4,3,2,1,0:T(8,128)(2,1)S(1)} async-done(((bf16[4,1,24,96,96]{4,3,2,1,0:T(8,128)(2,1)}), bf16[4,1,24,96,96]{4,3,2,1,0:T(8,128)(2,1)S(1)}, u32[]{:S(2)}, u32[]{:S(2)}) %all-to-all-start.2) | async-done | bytes 1769504 | tf_op jit(solution)/shard_map/all_to_all | solution.py:89
  167.5 3.9 all-to-all-start.4
  171.4 5.6 %convert_bitcast_fusion.8 = bf16[96,96,96]{1,2,0:T(8,128)(2,1)} fusion(bf16[96,96,1]{1,0,2:T(8,128)(2,1)S(1)} %copy-done.6, bf16[96,96,96]{2,1,0:T(8,128)(2,1)} %bitcast.213), kind=kOutput, calls=%fused_computation.49 | convolution fusion | flops 341508096 | bytes 3557376 | tf_op jit(solution)/shard_map/cy,pxyz->pxcz/dot_general | solution.py:44
  177.0 6.7 %copy.12 = bf16[96,96,96]{0,2,1:T(8,128)(2,1)} copy(bf16[96,96,96]{1,2,0:T(8,128)(2,1)} %convert_bitcast_fusion.8) | data formatting | bytes 3538944 | tf_op jit(solution)/shard_map/reshape.17
  183.7 4.7 convert_bitcast_fusion.7
  188.4 6.7 %copy.13 = bf16[96,96,96]{1,2,0:T(8,128)(2,1)} copy(bf16[96,96,96]{0,2,1:T(8,128)(2,1)} %convert_bitcast_fusion.7) | data formatting | bytes 3538944 | tf_op jit(solution)/shard_map/reshape.21
  195.2 4.6 convert_bitcast_fusion.6
  201.3 4.2 all-to-all-start.1
  205.4 5.6 %convert_bitcast_fusion.5 = bf16[96,96,96]{1,2,0:T(8,128)(2,1)} fusion(bf16[96,96,1]{1,0,2:T(8,128)(2,1)S(1)} %copy-done.6, bf16[96,96,96]{2,1,0:T(8,128)(2,1)} %bitcast.212), kind=kOutput, calls=%fused_computation.43 | convolution fusion | flops 341508096 | bytes 3557376 | tf_op jit(solution)/shard_map/cy,pxyz->pxcz/dot_general | solution.py:44
  211.1 6.7 %copy.16 = bf16[96,96,96]{0,2,1:T(8,128)(2,1)} copy(bf16[96,96,96]{1,2,0:T(8,128)(2,1)} %convert_bitcast_fusion.5) | data formatting | bytes 3538944 | tf_op jit(solution)/shard_map/reshape.36
  217.8 4.7 %convert_bitcast_fusion.4 = bf16[96,96,96]{0,2,1:T(8,128)(2,1)} fusion(bf16[96,96,1]{1,0,2:T(8,128)(2,1)S(1)} %copy-done.6, f32[96]{0:T(128)S(1)} %fusion.68, f32[96,96]{0,1:T(8,128)S(1)} %get-tuple-element.19, f32[96]{0:T(128)S(1)} %fusion.66, f32[96,96]{0,1:T(8,128)S(1)} %get-tuple-element.20, bf16[96,96,96]{0,2,1:T(8,128)(2,1)} %copy.16), kind=kOutput, calls=%fused_computation.42 | convolution fusion | flops 346816512 | bytes 3631872 | tf_op jit(solution)/shard_map/cx,pcyz->pxyz/dot_general | solution.py:44
  222.5 6.7 %copy.17 = bf16[96,96,96]{1,2,0:T(8,128)(2,1)} copy(bf16[96,96,96]{0,2,1:T(8,128)(2,1)} %convert_bitcast_fusion.4) | data formatting | bytes 3538944 | tf_op jit(solution)/shard_map/reshape.40
  229.3 4.7 convert_bitcast_fusion.3
  233.9 4.7 all-to-all-start.3
  238.6 5.6 %convert_bitcast_fusion.2 = bf16[96,96,96]{1,2,0:T(8,128)(2,1)} fusion(bf16[96,96,1]{1,0,2:T(8,128)(2,1)S(1)} %copy-done.6, bf16[96,96,96]{2,1,0:T(8,128)(2,1)} %bitcast.211), kind=kOutput, calls=%fused_computation.37 | convolution fusion | flops 341508096 | bytes 3557376 | tf_op jit(solution)/shard_map/cy,pxyz->pxcz/dot_general | solution.py:44
  244.2 6.7 %copy.20 = bf16[96,96,96]{0,2,1:T(8,128)(2,1)} copy(bf16[96,96,96]{1,2,0:T(8,128)(2,1)} %convert_bitcast_fusion.2) | data formatting | bytes 3538944 | tf_op jit(solution)/shard_map/reshape.55
  250.9 4.7 convert_bitcast_fusion.1
  255.6 6.7 %copy.21 = bf16[96,96,96]{1,2,0:T(8,128)(2,1)} copy(bf16[96,96,96]{0,2,1:T(8,128)(2,1)} %convert_bitcast_fusion.1) | data formatting | bytes 3538944 | tf_op jit(solution)/shard_map/reshape.59
  262.3 4.6 convert_bitcast_fusion
  267.2 32.2 %all_to_all.25 = bf16[1,1,96,96,96]{4,3,1,0,2:T(8,128)(2,1)S(1)} all-to-all(bf16[1,1,96,96,96]{4,3,1,0,2:T(8,128)(2,1)} %convert_bitcast_fusion), channel_id=1, replica_groups=mesh['band'=64,'grid'=4] {'grid'}, dimensions={2} | all-to-all | bytes 3538944 | tf_op jit(solution)/shard_map/all_to_all | solution.py:94
  299.5 5.8 %multiply_reduce_fusion.4 = (bf16[24,96,96,2]{2,1,0,3:T(8,128)(2,1)}, bf16[24,96,96,2]{2,1,0,3:T(8,128)(2,1)}, bf16[24,96,96,2]{2,1,0,3:T(8,128)(2,1)S(1)}) fusion(bf16[24,96,96,2,2]{2,1,0,4,3:T(8,128)(2,1)S(1)} %bitcast.207, f32[24,96,96,2]{2,1,0,3:T(8,128)S(1)} %copy-done.1, bf16[24,96,96,2,2]{2,1,0,4,3:T(8,128)(2,1)} %bitcast.6, ...), kind=kLoop, calls=%fused_computation.10 | loop fusion | flops 6635520 | bytes 9732096 | tf_op jit(solution)/shard_map/ijxyz,ixyz->jxyz/dot_general | solution.py:100
  305.3 7.5 %collective-permute-start.1 = (bf16[2,24,96,96]{3,2,1,0:T(8,128)(2,1)}, bf16[2,24,96,96]{3,2,1,0:T(8,128)(2,1)S(1)}, u32[]{:S(2)}, u32[]{:S(2)}) collective-permute-start(bf16[2,24,96,96]{3,2,1,0:T(8,128)(2,1)} %bitcast.179), channel_id=1, source_target_pairs={{0,252},{4,0},{8,4},{12,8},{16,12},{20,16},{24,20},{28,24},{32,28}... | collective-permute-start | bytes 2654216 | tf_op jit(solution)/shard_map/ppermute | solution.py:16
  313.0 2.9 multiply_reduce_fusion.3
  318.4 31.5 %collective-permute-done.1 = bf16[2,24,96,96]{3,2,1,0:T(8,128)(2,1)S(1)} collective-permute-done((bf16[2,24,96,96]{3,2,1,0:T(8,128)(2,1)}, bf16[2,24,96,96]{3,2,1,0:T(8,128)(2,1)S(1)}, u32[]{:S(2)}, u32[]{:S(2)}) %collective-permute-start.1) | collective-permute-done | bytes 884768 | tf_op jit(solution)/shard_map/ppermute | solution.py:16
  349.9 43.1 %collective-permute-done.3 = bf16[2,24,96,96]{3,2,1,0:T(8,128)(2,1)S(1)} collective-permute-done((bf16[2,24,96,96]{3,2,1,0:T(8,128)(2,1)}, bf16[2,24,96,96]{3,2,1,0:T(8,128)(2,1)S(1)}, u32[]{:S(2)}, u32[]{:S(2)}) %collective-permute-start.3) | collective-permute-done | bytes 884768 | tf_op jit(solution)/shard_map/ppermute | solution.py:16
  393.0 71.2 %collective-permute-done.5 = bf16[2,24,96,96]{3,2,1,0:T(8,128)(2,1)S(1)} collective-permute-done((bf16[2,24,96,96]{3,2,1,0:T(8,128)(2,1)S(1)}, bf16[2,24,96,96]{3,2,1,0:T(8,128)(2,1)S(1)}, u32[]{:S(2)}, u32[]{:S(2)}) %collective-permute-start.5) | collective-permute-done | bytes 884768 | tf_op jit(solution)/shard_map/ppermute | solution.py:16
  (33 shorter events, 20.5 us)
Async XLA Ops:
  3.5 27.7 %collective-permute-start = (bf16[2,24,96,96]{3,2,1,0:T(8,128)(2,1)S(1)}, bf16[2,24,96,96]{3,2,1,0:T(8,128)(2,1)S(1)}, u32[]{:S(2)}, u32[]{:S(2)}) collective-permute-start(bf16[2,24,96,96]{3,2,1,0:T(8,128)(2,1)S(1)} %get-tuple-element.9), channel_id=1, source_target_pairs={{0,4},{4,8},{8,12},{12,16},{16,20},{20,24},{24,28},{28,32},{32,36}... | collective-permute-start | bytes 2654216 | tf_op jit(solution)/shard_map/ppermute | solution.py:16
  31.2 34.5 %collective-permute-start.2 = (bf16[2,24,96,96]{3,2,1,0:T(8,128)(2,1)S(1)}, bf16[2,24,96,96]{3,2,1,0:T(8,128)(2,1)S(1)}, u32[]{:S(2)}, u32[]{:S(2)}) collective-permute-start(bf16[2,24,96,96]{3,2,1,0:T(8,128)(2,1)S(1)} %collective-permute-done), channel_id=1, source_target_pairs={{0,4},{4,8},{8,12},{12,16},{16,20},{20,24},{24,28},{28,32},{32,36}... | collective-permute-start | bytes 2654216 | tf_op jit(solution)/shard_map/ppermute | solution.py:16
  65.7 32.0 %collective-permute-start.4 = (bf16[2,24,96,96]{3,2,1,0:T(8,128)(2,1)S(1)}, bf16[2,24,96,96]{3,2,1,0:T(8,128)(2,1)S(1)}, u32[]{:S(2)}, u32[]{:S(2)}) collective-permute-start(bf16[2,24,96,96]{3,2,1,0:T(8,128)(2,1)S(1)} %collective-permute-done.2), channel_id=1, source_target_pairs={{0,4},{4,8},{8,12},{12,16},{16,20},{20,24},{24,28},{28,32},{32,36}... | collective-permute-start | bytes 2654216 | tf_op jit(solution)/shard_map/ppermute | solution.py:16
  133.9 32.1 %all-to-all-start.2 = ((bf16[4,1,24,96,96]{4,3,2,1,0:T(8,128)(2,1)}), bf16[4,1,24,96,96]{4,3,2,1,0:T(8,128)(2,1)S(1)}, u32[]{:S(2)}, u32[]{:S(2)}) async-start(bf16[4,1,24,96,96]{4,3,2,1,0:T(8,128)(2,1)} %bitcast.215), calls=%async_computation.2 | async-start | bytes 4718592 | tf_op jit(solution)/shard_map/all_to_all | solution.py:89
  166.0 1.5 copy-start.5
  166.0 5.4 %copy-start.6 = (bf16[96,96,1]{1,0,2:T(8,128)(2,1)S(1)}, bf16[96,96,1]{1,0,2:T(8,128)(2,1)}, u32[]{:S(2)}) copy-start(bf16[96,96,1]{1,0,2:T(8,128)(2,1)} %constant.27) | copy-start | bytes 55300
  167.5 32.4 %all-to-all-start.4 = ((bf16[4,1,24,96,96]{4,3,2,1,0:T(8,128)(2,1)}), bf16[4,1,24,96,96]{4,3,2,1,0:T(8,128)(2,1)S(1)}, u32[]{:S(2)}, u32[]{:S(2)}) async-start(bf16[4,1,24,96,96]{4,3,2,1,0:T(8,128)(2,1)} %bitcast.214), calls=%async_computation.4 | async-start | bytes 4718592 | tf_op jit(solution)/shard_map/all_to_all | solution.py:89
  199.9 1.4 copy-start.4
  201.3 32.7 %all-to-all-start.1 = ((bf16[1,1,96,96,96]{4,3,1,0,2:T(8,128)(2,1)}), bf16[1,1,96,96,96]{4,3,1,0,2:T(8,128)(2,1)S(1)}, u32[]{:S(2)}, u32[]{:S(2)}) async-start(bf16[1,1,96,96,96]{4,3,1,0,2:T(8,128)(2,1)} %convert_bitcast_fusion.6), calls=%async_computation.1 | async-start | bytes 4718592 | tf_op jit(solution)/shard_map/all_to_all | solution.py:94
  233.9 33.3 %all-to-all-start.3 = ((bf16[1,1,96,96,96]{4,3,1,0,2:T(8,128)(2,1)}), bf16[1,1,96,96,96]{4,3,1,0,2:T(8,128)(2,1)}, u32[]{:S(2)}, u32[]{:S(2)}) async-start(bf16[1,1,96,96,96]{4,3,1,0,2:T(8,128)(2,1)} %convert_bitcast_fusion.3), calls=%async_computation.3 | async-start | bytes 4718592 | tf_op jit(solution)/shard_map/all_to_all | solution.py:94
  267.2 32.2 %copy-start.1 = (f32[24,96,96,2]{2,1,0,3:T(8,128)S(1)}, f32[24,96,96,2]{2,1,0,3:T(8,128)}, u32[]{:S(2)}) copy-start(f32[24,96,96,2]{2,1,0,3:T(8,128)} %get-tuple-element.8) | copy-start | bytes 5308420
  299.5 13.5 %copy-start.2 = (f32[24,96,96,2]{2,1,0,3:T(8,128)S(1)}, f32[24,96,96,2]{2,1,0,3:T(8,128)}, u32[]{:S(2)}) copy-start(f32[24,96,96,2]{2,1,0,3:T(8,128)} %get-tuple-element.15) | copy-start | bytes 5308420
  305.3 44.6 %collective-permute-start.1 = (bf16[2,24,96,96]{3,2,1,0:T(8,128)(2,1)}, bf16[2,24,96,96]{3,2,1,0:T(8,128)(2,1)S(1)}, u32[]{:S(2)}, u32[]{:S(2)}) collective-permute-start(bf16[2,24,96,96]{3,2,1,0:T(8,128)(2,1)} %bitcast.179), channel_id=1, source_target_pairs={{0,252},{4,0},{8,4},{12,8},{16,12},{20,16},{24,20},{28,24},{32,28}... | collective-permute-start | bytes 2654216 | tf_op jit(solution)/shard_map/ppermute | solution.py:16
  312.8 80.2 %collective-permute-start.3 = (bf16[2,24,96,96]{3,2,1,0:T(8,128)(2,1)}, bf16[2,24,96,96]{3,2,1,0:T(8,128)(2,1)S(1)}, u32[]{:S(2)}, u32[]{:S(2)}) collective-permute-start(bf16[2,24,96,96]{3,2,1,0:T(8,128)(2,1)} %bitcast.178), channel_id=1, source_target_pairs={{0,248},{4,252},{8,0},{12,4},{16,8},{20,12},{24,16},{28,20},{32,24... | collective-permute-start | bytes 2654216 | tf_op jit(solution)/shard_map/ppermute | solution.py:16
  312.8 151.5 %collective-permute-start.5 = (bf16[2,24,96,96]{3,2,1,0:T(8,128)(2,1)S(1)}, bf16[2,24,96,96]{3,2,1,0:T(8,128)(2,1)S(1)}, u32[]{:S(2)}, u32[]{:S(2)}) collective-permute-start(bf16[2,24,96,96]{3,2,1,0:T(8,128)(2,1)S(1)} %bitcast.217), channel_id=1, source_target_pairs={{0,244},{4,248},{8,252},{12,0},{16,4},{20,8},{24,12},{28,16},{32,2... | collective-permute-start | bytes 2654216 | tf_op jit(solution)/shard_map/ppermute | solution.py:16
  313.0 2.9 copy-start.3
  315.9 1.7 copy-start
where the time goes:
time: 472 us; the launch traced here: 467 us
  waiting for transfers between devices  261 us (55%)
  blocking collectives  64 us (14%)
  matrix products  44.7 us (9%)
  local copies, waits for them, and re-layouts  44.3 us (9%)
  starting transfers between devices  27.9 us (6%)
  other arithmetic  24.6 us (5%)
    ppermute x6, waiting for transfers between devices, passed_along(): lax.ppermute(value, axis, [(i, (i + by) % length) for i in range(length)])  232 us
    dot_general x9, matrix products, apply_table(): return jnp.einsum(form, cosines, data, preferred_element_type=jnp.float32)  44.7 us
    another operation x6, local copies, waits for them, and re-layouts  40.4 us
    all_to_all x1, blocking collectives, per_device(): lax.all_to_all(potential, 'grid', split_axis=2, concat_axis=0, tiled=True)  32.2 us
    all_to_all x1, blocking collectives, per_device(): lax.all_to_all(grouped, 'grid', split_axis=0, concat_axis=2, tiled=True)  31.8 us
    all_to_all x2, waiting for transfers between devices, per_device(): lax.all_to_all(grouped, 'grid', split_axis=0, concat_axis=2, tiled=True)  28.5 us
    ppermute x6, starting transfers between devices, passed_along(): lax.ppermute(value, axis, [(i, (i + by) % length) for i in range(length)])  11.5 us
  transfers between devices with their start and end apart: 10, of which 9 were waited for; matrix products, arithmetic and copies ran while one was open for 20% of the time, Pallas kernels for 0%

commit v1 on v0

v1 whole, which is shorter than its diff:
```python
import functools

import jax
import jax.numpy as jnp
import numpy as np
from jax import lax
from jax.experimental import pallas as pl
from jax.experimental.pallas import tpu as pltpu
from jax.sharding import PartitionSpec as P


NG = 96
PAIRS = 12
ROWS = 144
THIRD = 48
LANES = 128
SLAB = PAIRS * ROWS
KERNEL_SCALE = 16.0
SCREEN_SQ = 0.05
AXES = ("band", "grid")
BF = jnp.bfloat16
F32 = jnp.float32
UNROLL = 2


def dft_table(length):
    half = length // 2
    rows = np.arange(length)
    freq = np.where(rows <= half, rows, rows - half)
    phase = 2.0 * np.pi * np.outer(freq, rows) / length
    return np.where((rows <= half)[:, None], np.cos(phase), np.sin(phase))


def z_tables():
    table = dft_table(NG)
    forward = np.zeros((3, LANES, 2 * LANES))
    inverse = np.zeros((3, 2 * LANES, LANES))
    for g in range(3):
        part = table[:, 32 * g : 32 * g + 32]
        forward[g, :NG, :NG] = table.T
        forward[g, NG:, LANES : LANES + NG] = part.T
        inverse[g, :NG, :NG] = table
        inverse[g, LANES : LANES + NG, NG:] = part
    return jnp.asarray(forward, BF), jnp.asarray(inverse, BF)


def multiplier():
    index = np.arange(NG)
    freq = np.where(index <= NG // 2, index, index - NG // 2).astype(np.float32)
    weight = (np.where((index == 0) | (index == NG // 2), 1.0, 2.0) / NG).astype(np.float32)
    lane_freq = jnp.asarray(np.pad(freq, (0, LANES - NG)))
    lane_weight = jnp.asarray(np.pad(weight, (0, LANES - NG)))
    freq, weight = jnp.asarray(freq), jnp.asarray(weight)
    freq_b, weight_b = freq.reshape(48, 1, 2, 1), weight.reshape(48, 1, 2, 1)
    square = freq[None, :, None, None] ** 2 + freq_b**2 + lane_freq**2
    scale = weight[None, :, None, None] * weight_b * lane_weight
    return (KERNEL_SCALE * scale / (square + SCREEN_SQ)).reshape(48 * NG, 2 * LANES)


def dot(left, right):
    return jnp.dot(left, right, preferred_element_type=F32)


def pack_kernel(place, bands, *outs):
    high, core = place[0], place[1]
    mix = high ^ core
    for p in range(bands.shape[1] // 2):
        packed = []
        for band in range(2):
            first, second = bands[band, 2 * p], bands[band, 2 * p + 1]
            heads = (first[:THIRD], first[THIRD:], second[:THIRD])
            packed.append(
                jnp.concatenate(
                    [
                        jnp.concatenate([heads[g], second[THIRD:, 32 * g : 32 * g + 32]], axis=1)
                        for g in range(3)
                    ],
                    axis=0,
                )
            )
        for n, flag in enumerate((core, mix, high)):
            same, other = (
                jnp.where(flag == 0, packed[0], packed[1]),
                jnp.where(flag == 0, packed[1], packed[0]),
            )
            outs[2 * n][pl.ds(p * ROWS, ROWS)] = same.astype(BF)
            outs[2 * n + 1][pl.ds(p * ROWS, ROWS)] = other.astype(BF)


def pack(place, bands):
    steps = 3
    per = PAIRS // steps
    return pl.pallas_call(
        pack_kernel,
        grid=(steps,),
        in_specs=[
            pl.BlockSpec(memory_space=pltpu.SMEM),
            pl.BlockSpec((2, 2 * per, NG, NG), lambda i: (0, i, 0, 0)),
        ],
        out_specs=[pl.BlockSpec((per * ROWS, LANES), lambda i: (i, 0))] * 6,
        out_shape=[jax.ShapeDtypeStruct((SLAB, LANES), BF)] * 6,
        compiler_params=pltpu.CompilerParams(vmem_limit_bytes=48 << 20),
        name="pack",
    )(place, bands)


def unpack_kernel(place, *refs):
    a0, a1, a2, a3, b0, b1, b2, b3, c0, c2, out = refs
    high, core = place[0], place[1]
    mix = high ^ core
    for p in range(out.shape[1] // 2):
        rows = pl.ds(p * ROWS, ROWS)
        load = lambda ref: ref[rows].astype(F32)
        terms = (
            (core, load(a0) + load(a2), load(a1) + load(a3)),
            (mix, load(b0) + load(b3), load(b1) + load(b2)),
            (high, load(c0), load(c2)),
        )
        for band in range(2):
            total = sum(jnp.where(flag == band, same, other) for flag, same, other in terms)
            total = -total
            out[band, 2 * p] = total[: 2 * THIRD, :NG]
            tail = [total[THIRD * g : THIRD * g + THIRD, NG:] for g in range(3)]
            out[band, 2 * p + 1, :THIRD] = total[2 * THIRD :, :NG]
            out[band, 2 * p + 1, THIRD:] = jnp.concatenate(tail, axis=1)


def unpack(place, parts):
    steps = 3
    per = PAIRS // steps
    return pl.pallas_call(
        unpack_kernel,
        grid=(steps,),
        in_specs=[pl.BlockSpec(memory_space=pltpu.SMEM)]
        + [pl.BlockSpec((per * ROWS, LANES), lambda i: (i, 0))] * 10,
        out_specs=pl.BlockSpec((2, 2 * per, NG, NG), lambda i: (0, i, 0, 0)),
        out_shape=jax.ShapeDtypeStruct((2, 2 * PAIRS, NG, NG), F32),
        compiler_params=pltpu.CompilerParams(vmem_limit_bytes=48 << 20),
        name="unpack",
    )(place, *parts)


def transform(left, right, tables, grid_values, emit):
    y_table, y_back, x_table, x_back, z_table, z_back, weights = tables

    for r in range(4):

        def forward(p, carry, r=r):
            rows = pl.ds(pl.multiple_of(p * ROWS, ROWS), ROWS)
            density = left[r][rows] * right[r][rows]
            parts = [dot(density[THIRD * g : THIRD * g + THIRD], z_table[g]) for g in range(3)]
            one = jnp.concatenate([parts[0][:, :LANES], parts[1][:, :LANES]], axis=0)
            tail = parts[0][:, LANES:] + parts[1][:, LANES:] + parts[2][:, LANES:]
            two = jnp.concatenate([parts[2][:, :LANES], tail], axis=0)
            lines = dot(y_table[...], jnp.concatenate([one, two], axis=1).astype(BF))
            x = r * 2 * PAIRS + 2 * p
            grid_values[pl.ds(x, NG, stride=NG), :] = lines[:, :LANES]
            grid_values[pl.ds(x + 1, NG, stride=NG), :] = lines[:, LANES:]
            return carry

        lax.fori_loop(0, PAIRS, forward, 0, unroll=UNROLL)

    def middle(q, carry):
        upper = pl.ds(pl.multiple_of(q * 2 * NG, 2 * NG), NG)
        lower = pl.ds(pl.multiple_of(q * 2 * NG + NG, NG), NG)
        block = jnp.concatenate([grid_values[upper, :], grid_values[lower, :]], axis=1).astype(BF)
        scaled = weights[pl.ds(pl.multiple_of(q * NG, NG), NG), :] * dot(x_table[...], block)
        back = dot(x_back[...], scaled.astype(BF))
        grid_values[upper, :] = back[:, :LANES]
        grid_values[lower, :] = back[:, LANES:]
        return carry

    lax.fori_loop(0, NG // 2, middle, 0, unroll=2 * UNROLL)

    for r in range(4):

        def inverse(p, carry, r=r):
            x = r * 2 * PAIRS + 2 * p
            one = grid_values[pl.ds(x, NG, stride=NG), :]
            two = grid_values[pl.ds(x + 1, NG, stride=NG), :]
            lines = dot(y_back[...], jnp.concatenate([one, two], axis=1).astype(BF)).astype(BF)
            one, two = lines[:, :LANES], lines[:, LANES:]
            heads = (one[:THIRD], one[THIRD:], two[:THIRD])
            potential = jnp.concatenate(
                [
                    dot(jnp.concatenate([heads[g], two[THIRD:]], axis=1), z_back[g])
                    for g in range(3)
                ],
                axis=0,
            ).astype(BF)
            emit(r, pl.ds(pl.multiple_of(p * ROWS, ROWS), ROWS), potential)
            return carry

        lax.fori_loop(0, PAIRS, inverse, 0, unroll=UNROLL)


def first_kernel(*refs):
    tables, refs = refs[:7], refs[7:]
    a, b, field_ab, grid_values = refs[:4], refs[4:8], refs[8:12], refs[12]

    def emit(r, rows, potential):
        field_ab[r][rows] = potential

    transform(a, b, tables, grid_values, emit)


def second_kernel(*refs):
    tables, refs = refs[:7], refs[7:]
    a, b, c, field_ab = refs[:4], refs[4:8], refs[8:12], refs[12:16]
    field_ac, out_a, grid_values = refs[16:20], refs[20:24], refs[24]

    def emit(r, rows, potential):
        field_ac[r][rows] = potential
        total = field_ab[r][rows].astype(F32) * b[r][rows].astype(F32)
        total += potential.astype(F32) * c[r][rows].astype(F32)
        out_a[r][rows] = total.astype(BF)

    transform(a, c, tables, grid_values, emit)


def third_kernel(*refs):
    tables, refs = refs[:7], refs[7:]
    a, b, c, field_ab, field_ac = (refs[4 * n : 4 * n + 4] for n in range(5))
    out_b, out_keep, out_give, grid_values = refs[20:24], refs[24], refs[25], refs[26]

    def emit(r, rows, potential):
        field = potential.astype(F32)
        one, two, three = (v[r][rows].astype(F32) for v in (a, b, c))
        out_b[r][rows] = (field_ab[r][rows].astype(F32) * one + field * three).astype(BF)
        total = (field_ac[r][rows].astype(F32) * one + field * two).astype(BF)
        target = (out_keep, out_give)[r % 2]
        target[pl.ds(pl.multiple_of(rows.start + (r // 2) * SLAB, ROWS), ROWS)] = total

    transform(b, c, tables, grid_values, emit)


def call_transform(kernel, name, tables, slabs, out_slabs):
    flops = 2 * 6 * NG**4
    return pl.pallas_call(
        kernel,
        in_specs=[pl.BlockSpec(memory_space=pltpu.VMEM)] * (7 + len(slabs)),
        out_specs=[pl.BlockSpec(memory_space=pltpu.VMEM)] * len(out_slabs),
        out_shape=[jax.ShapeDtypeStruct((n * SLAB, LANES), BF) for n in out_slabs],
        scratch_shapes=[pltpu.VMEM((NG * NG, LANES), F32)],
        compiler_params=pltpu.CompilerParams(vmem_limit_bytes=50 << 20),
        cost_estimate=pl.CostEstimate(flops=flops * 10, bytes_accessed=12 << 20, transcendentals=0),
        name=name,
    )(*tables, *slabs)


def sum_kernel(kept, received, *outs):
    total = (kept[...].astype(F32) + received[...].astype(F32)).astype(BF)
    outs[0][...] = total[:SLAB]
    outs[1][...] = total[SLAB:]


def add_halves(kept, received):
    return pl.pallas_call(
        sum_kernel,
        in_specs=[pl.BlockSpec(memory_space=pltpu.VMEM)] * 2,
        out_specs=[pl.BlockSpec(memory_space=pltpu.VMEM)] * 2,
        out_shape=[jax.ShapeDtypeStruct((SLAB, LANES), BF)] * 2,
        name="add_halves",
    )(kept, received)


def passed(value, blocks, by, length):
    pairs = [
        (4 * k + s, 4 * ((k + by) % length) + (s ^ blocks)) for k in range(length) for s in range(4)
    ]
    return lax.ppermute(value, AXES, pairs)


def per_device(bands):
    length = lax.axis_size("band")
    me = lax.axis_index("grid")
    place = jnp.stack([me // 2, me % 2]).astype(jnp.int32)
    send = functools.partial(passed, length=length)

    core_same, core_other, mix_same, mix_other, high_same, high_other = pack(place, bands)
    c = [send(high_same, 0, 2), None, send(high_other, 2, 2), None]
    b = [mix_same, send(mix_other, 1, 0), send(mix_other, 2, 0), send(mix_same, 3, 0)]
    a = [send((core_same, core_other)[r % 2], r, -1) for r in range(4)]
    c[1], c[3] = send(c[0], 1, 0), send(c[2], 1, 0)

    table = dft_table(NG)
    orders = [np.concatenate([np.arange(24) + 24 * (r ^ s) for r in range(4)]) for s in range(4)]
    x_tables = jnp.asarray(np.stack([table[:, order] for order in orders]), BF)
    x_table = lax.dynamic_index_in_dim(x_tables, me, 0, keepdims=False)
    x_backs = jnp.asarray(np.stack([table[:, order].T for order in orders]), BF)
    x_back = lax.dynamic_index_in_dim(x_backs, me, 0, keepdims=False)
    y_table, y_back = jnp.asarray(table, BF), jnp.asarray(table.T, BF)
    z_table, z_back = z_tables()
    tables = (y_table, y_back, x_table, x_back, z_table, z_back, multiplier())

    field_ab = call_transform(first_kernel, "pair_ab", tables, [*a, *b], [1] * 4)
    outs = call_transform(second_kernel, "pair_ac", tables, [*a, *b, *c, *field_ab], [1] * 8)
    field_ac, out_a = outs[:4], outs[4:]
    back_a = [send(out_a[r], r, 1) for r in range(4)]
    outs = call_transform(
        third_kernel, "pair_bc", tables, [*a, *b, *c, *field_ab, *field_ac], [1] * 4 + [2] * 2
    )
    out_b, kept, given = outs[:4], outs[4], outs[5]
    c0, c2 = add_halves(kept, send(given, 1, 0))
    back_c = [send(c0, 0, -2), send(c2, 2, -2)]
    back_b = [out_b[0]] + [send(out_b[r], r, 0) for r in range(1, 4)]
    return unpack(place, [*back_a, *back_b, *back_c])


def solution(mesh):
    spec = P("band", "grid", None, None)
    return jax.shard_map(
        per_device, mesh=mesh, in_specs=(spec,), out_specs=spec, check_vma=False
    )
```

time: 472 us -> 290 us (0.61)
  waiting for transfers between devices: 261 us -> 99.9 us
  Pallas kernels: 0 us -> 113 us
  blocking collectives: 64 us -> 0 us
  matrix products: 44.7 us -> 0 us
  other arithmetic: 24.6 us -> 4.64 us
  local copies, waits for them, and re-layouts: 44.3 us -> 25.4 us
  starting transfers between devices: 27.9 us -> 43.1 us
    ppermute x6 -> x21, waiting for transfers between devices: 232 us -> 99.9 us  [passed(): return lax.ppermute(value, AXES, pairs)]
    pallas_call x0 -> x6, Pallas kernels: none -> 113 us  [the longest x3 106 us: call_transform(): pl.pallas_call(kernel, in_specs=[pl.BlockSpec(memory_space=pltpu.VMEM)] *...]
    all_to_all x2 -> x0, blocking collectives: 64 us -> none  [the longest x1 32.2 us: per_device(): lax.all_to_all(potential, 'grid', split_axis=2, concat_axis=0, tiled=True)]
    dot_general x9 -> x0, matrix products: 44.7 us -> none  [apply_table(): return jnp.einsum(form, cosines, data, preferred_element_type=jnp.float32)]
    another operation x6 -> x0, local copies, waits for them, and re-layouts: 40.4 us -> none
    ppermute x6 -> x21, starting transfers between devices: 11.5 us -> 43.1 us  [passed(): return lax.ppermute(value, AXES, pairs)]
    all_to_all x4 -> x0, waiting for transfers between devices: 28.7 us -> none  [the longest x2 28.5 us: per_device(): lax.all_to_all(grouped, 'grid', split_axis=0, concat_axis=2, tiled=True)]
    all_to_all x4 -> x0, starting transfers between devices: 16.4 us -> none  [the longest x2 8.82 us: per_device(): lax.all_to_all(potential, 'grid', split_axis=2, concat_axis=0, tiled=True)]
  transfers between devices with their start and end apart: 10 -> 21, of which waited for: 9 -> 12; matrix products, arithmetic and copies ran while one was open for 20% -> 6% of each run, Pallas kernels for 0% -> 13%
where the time goes in v1:
time: 290 us; the launch traced here: 286 us
  Pallas kernels  113 us (39%)
  waiting for transfers between devices  99.9 us (34%)
  starting transfers between devices  43.1 us (15%)
  local copies, waits for them, and re-layouts  25.4 us (9%)
  other arithmetic  4.64 us (2%)
    pallas_call x3, Pallas kernels, call_transform(): pl.pallas_call(kernel, in_specs=[pl.BlockSpec(memory_space=pltpu.VMEM)] *...  106 us
    ppermute x21, waiting for transfers between devices, passed(): return lax.ppermute(value, AXES, pairs)  99.9 us
    ppermute x21, starting transfers between devices, passed(): return lax.ppermute(value, AXES, pairs)  43.1 us
    unnamed x58, local copies, waits for them, and re-layouts  13.1 us
  transfers between devices with their start and end apart: 21, of which 12 were waited for; matrix products, arithmetic and copies ran while one was open for 6% of the time, Pallas kernels for 13%

profile of v1, /device:TPU:32, one launch (start us, length us, event | category | flops | bytes accessed | tf_op | source)
XLA Modules:
  0.0 286.3 jit_solution(4258671863450694932)
XLA Ops:
  0.1 1.7 copy-done
  1.8 1.3 pack.1
  3.1 1.9 collective-permute-start
  5.0 9.1 %collective-permute-start.2 = (bf16[1728,128]{1,0:T(8,128)(2,1)S(1)}, bf16[1728,128]{1,0:T(8,128)(2,1)S(1)}, u32[]{:S(2)}, u32[]{:S(2)}) collective-permute-start(bf16[1728,128]{1,0:T(8,128)(2,1)S(1)} %get-tuple-element.31), channel_id=1, source_target_pairs={{0,254},{1,255},{2,252},{3,253},{4,2},{5,3},{6,0},{7,1},{8,6},{9,7... | collective-permute-start | bytes 1327112 | tf_op jit(solution)/shard_map/ppermute | solution.py:271
  14.1 1.9 collective-permute-start.3
  16.0 1.1 broadcast_add_fusion
  17.5 2.0 collective-permute-start.5
  19.5 14.7 %collective-permute-done.1.refs_8_ = bf16[1728,128]{1,0:T(8,128)(2,1)S(1)} collective-permute-done((bf16[1728,128]{1,0:T(8,128)(2,1)S(1)}, bf16[1728,128]{1,0:T(8,128)(2,1)S(1)}, u32[]{:S(2)}, u32[]{:S(2)}) %collective-permute-start.1) | collective-permute-done | bytes 442400 | tf_op jit(solution)/shard_map/ppermute | solution.py:271
  34.2 2.3 collective-permute-start.6
  36.5 4.5 %collective-permute-start.7 = (bf16[1728,128]{1,0:T(8,128)(2,1)S(1)}, bf16[1728,128]{1,0:T(8,128)(2,1)}, u32[]{:S(2)}, u32[]{:S(2)}) collective-permute-start(bf16[1728,128]{1,0:T(8,128)(2,1)S(1)} %get-tuple-element.35), channel_id=1, source_target_pairs={{0,8},{1,9},{2,10},{3,11},{4,12},{5,13},{6,14},{7,15},{8,16},{9,17... | collective-permute-start | bytes 1327112 | tf_op jit(solution)/shard_map/ppermute | solution.py:271
  41.0 2.9 %collective-permute-done.3.refs_10_ = bf16[1728,128]{1,0:T(8,128)(2,1)S(1)} collective-permute-done((bf16[1728,128]{1,0:T(8,128)(2,1)S(1)}, bf16[1728,128]{1,0:T(8,128)(2,1)S(1)}, u32[]{:S(2)}, u32[]{:S(2)}) %collective-permute-start.3) | collective-permute-done | bytes 442400 | tf_op jit(solution)/shard_map/ppermute | solution.py:271
  43.9 4.4 %collective-permute-start.9 = (bf16[1728,128]{1,0:T(8,128)(2,1)S(1)}, bf16[1728,128]{1,0:T(8,128)(2,1)}, u32[]{:S(2)}, u32[]{:S(2)}) collective-permute-start(bf16[1728,128]{1,0:T(8,128)(2,1)S(1)} %get-tuple-element.36), channel_id=1, source_target_pairs={{0,10},{1,11},{2,8},{3,9},{4,14},{5,15},{6,12},{7,13},{8,18},{9,19... | collective-permute-start | bytes 1327112 | tf_op jit(solution)/shard_map/ppermute | solution.py:271
  48.3 5.7 %add.60 = f32[48,96,2,128]{3,2,1,0:T(2,128)S(1)} broadcast(f32[48,96,2]{2,1,0:T(8,128)S(1)} %broadcast_add_fusion), dimensions={0,1,2} | broadcast | bytes 4755456 | tf_op jit(solution)/shard_map/add | solution.py:55
  54.0 5.8 %mul.51 = f32[48,96,2,128]{3,2,1,0:T(2,128)S(1)} broadcast(f32[48,96,2]{2,1,0:T(8,128)S(1)} %broadcast_multiply_fusion), dimensions={0,1,2} | broadcast | bytes 4755456 | tf_op jit(solution)/shard_map/mul | solution.py:56
  59.8 3.1 %fusion.1.refs_6_ = f32[4608,256]{1,0:T(8,128)} fusion(f32[576,8,2,128]{3,2,1,0:T(2,128)S(1)} %bitcast.26, f32[576,8,2,128]{3,2,1,0:T(2,128)S(1)} %bitcast.27, f32[256]{0:T(256)S(1)} %get-tuple-element.59, f32[256]{0:T(256)S(1)} %get-tuple-element.60), kind=kLoop, calls=%fused_computation.2 | loop fusion | flops 5898240 | bytes 14157824 | tf_op jit(solution)/shard_map/div | solution.py:57
  63.7 15.1 %collective-permute-done.7.refs_15_ = bf16[1728,128]{1,0:T(8,128)(2,1)} collective-permute-done((bf16[1728,128]{1,0:T(8,128)(2,1)S(1)}, bf16[1728,128]{1,0:T(8,128)(2,1)}, u32[]{:S(2)}, u32[]{:S(2)}) %collective-permute-start.7) | collective-permute-done | bytes 442400 | tf_op jit(solution)/shard_map/ppermute | solution.py:271
  78.8 8.4 %collective-permute-done.9.refs_17_ = bf16[1728,128]{1,0:T(8,128)(2,1)} collective-permute-done((bf16[1728,128]{1,0:T(8,128)(2,1)S(1)}, bf16[1728,128]{1,0:T(8,128)(2,1)}, u32[]{:S(2)}, u32[]{:S(2)}) %collective-permute-start.9) | collective-permute-done | bytes 442400 | tf_op jit(solution)/shard_map/ppermute | solution.py:271
  90.6 33.6 %pair_ab.1 = (bf16[1728,128]{1,0:T(8,128)(2,1)S(1)}, bf16[1728,128]{1,0:T(8,128)(2,1)S(1)}, bf16[1728,128]{1,0:T(8,128)(2,1)S(1)}, bf16[1728,128]{1,0:T(8,128)(2,1)S(1)}) custom-call(bf16[96,96]{1,0:T(8,128)(2,1)S(1)} %copy-done.12, bf16[96,96]{1,0:T(8,128)(2,1)S(1)} %copy-done.13, bf16[96,96]{1,0:T(8,128)(2,1)S(1)} %get-tuple-element.58.refs_2_, ...), custom_call_target="tpu_custom_call" | custom-call | flops 10192158720 | bytes 12582912 | tf_op jit(solution)/shard_map/pair_ab/pallas_call | solution.py:239
  128.4 36.1 %pair_ac.1 = (bf16[1728,128]{1,0:T(8,128)(2,1)S(1)}, bf16[1728,128]{1,0:T(8,128)(2,1)S(1)}, bf16[1728,128]{1,0:T(8,128)(2,1)S(1)}, bf16[1728,128]{1,0:T(8,128)(2...) custom-call(bf16[96,96]{1,0:T(8,128)(2,1)S(1)} %copy-done.12, ...), custom_call_target="tpu_custom_call" | custom-call | flops 10192158720 | bytes 12582912 | tf_op jit(solution)/shard_map/pair_ac/pallas_call | solution.py:239
  167.6 36.4 %pair_bc.1 = (bf16[1728,128]{1,0:T(8,128)(2,1)S(1)}, bf16[1728,128]{1,0:T(8,128)(2,1)}, bf16[1728,128]{1,0:T(8,128)(2,1)S(1)}, bf16[1728,128]{1,0:T(8,128)(2,1)S...) custom-call(bf16[96,96]{1,0:T(8,128)(2,1)S(1)} %copy-done.12, bf16[96,96]{1,0:T(8,128)(2,1)S(1)} %copy-done.13, ...), custom_call_target="tpu_custom_call" | custom-call | flops 10192158720 | bytes 12582912 | tf_op jit(solution)/shard_map/pair_bc/pallas_call | solution.py:239
  204.6 2.2 collective-permute-done.18.received
  206.8 1.0 copy-done.22
  208.1 2.5 add_halves.1
  210.6 9.9 %collective-permute-done.11.refs_0_ = bf16[1728,128]{1,0:T(8,128)(2,1)S(1)} collective-permute-done((bf16[1728,128]{1,0:T(8,128)(2,1)}, bf16[1728,128]{1,0:T(8,128)(2,1)S(1)}, u32[]{:S(2)}, u32[]{:S(2)}) %collective-permute-start.11) | collective-permute-done | bytes 442400 | tf_op jit(solution)/shard_map/ppermute | solution.py:271
  220.6 8.4 %collective-permute-done.12.refs_1_ = bf16[1728,128]{1,0:T(8,128)(2,1)S(1)} collective-permute-done((bf16[1728,128]{1,0:T(8,128)(2,1)}, bf16[1728,128]{1,0:T(8,128)(2,1)S(1)}, u32[]{:S(2)}, u32[]{:S(2)}) %collective-permute-start.12) | collective-permute-done | bytes 442400 | tf_op jit(solution)/shard_map/ppermute | solution.py:271
  229.3 9.3 %collective-permute-done.13.refs_2_ = bf16[1728,128]{1,0:T(8,128)(2,1)S(1)} collective-permute-done((bf16[1728,128]{1,0:T(8,128)(2,1)}, bf16[1728,128]{1,0:T(8,128)(2,1)S(1)}, u32[]{:S(2)}, u32[]{:S(2)}) %collective-permute-start.13) | collective-permute-done | bytes 442400 | tf_op jit(solution)/shard_map/ppermute | solution.py:271
  238.6 7.8 %collective-permute-start.19 = (bf16[1728,128]{1,0:T(8,128)(2,1)}, bf16[1728,128]{1,0:T(8,128)(2,1)S(1)}, u32[]{:S(2)}, u32[]{:S(2)}) collective-permute-start(bf16[1728,128]{1,0:T(8,128)(2,1)} %get-tuple-element.55), channel_id=1, source_target_pairs={{0,248},{1,249},{2,250},{3,251},{4,252},{5,253},{6,254},{7,255},{8... | collective-permute-start | bytes 1327112 | tf_op jit(solution)/shard_map/ppermute | solution.py:271
  247.1 7.9 %collective-permute-start.20 = (bf16[1728,128]{1,0:T(8,128)(2,1)}, bf16[1728,128]{1,0:T(8,128)(2,1)S(1)}, u32[]{:S(2)}, u32[]{:S(2)}) collective-permute-start(bf16[1728,128]{1,0:T(8,128)(2,1)} %get-tuple-element.56), channel_id=1, source_target_pairs={{0,250},{1,251},{2,248},{3,249},{4,254},{5,255},{6,252},{7,253},{8... | collective-permute-start | bytes 1327112 | tf_op jit(solution)/shard_map/ppermute | solution.py:271
  255.0 9.0 %collective-permute-done.17.refs_7_ = bf16[1728,128]{1,0:T(8,128)(2,1)S(1)} collective-permute-done((bf16[1728,128]{1,0:T(8,128)(2,1)S(1)}, bf16[1728,128]{1,0:T(8,128)(2,1)S(1)}, u32[]{:S(2)}, u32[]{:S(2)}) %collective-permute-start.17) | collective-permute-done | bytes 442400 | tf_op jit(solution)/shard_map/ppermute | solution.py:271
  264.0 12.3 %collective-permute-done.19.refs_8_ = bf16[1728,128]{1,0:T(8,128)(2,1)S(1)} collective-permute-done((bf16[1728,128]{1,0:T(8,128)(2,1)}, bf16[1728,128]{1,0:T(8,128)(2,1)S(1)}, u32[]{:S(2)}, u32[]{:S(2)}) %collective-permute-start.19) | collective-permute-done | bytes 442400 | tf_op jit(solution)/shard_map/ppermute | solution.py:271
  276.3 7.0 %collective-permute-done.20.refs_9_ = bf16[1728,128]{1,0:T(8,128)(2,1)S(1)} collective-permute-done((bf16[1728,128]{1,0:T(8,128)(2,1)}, bf16[1728,128]{1,0:T(8,128)(2,1)S(1)}, u32[]{:S(2)}, u32[]{:S(2)}) %collective-permute-start.20) | collective-permute-done | bytes 442400 | tf_op jit(solution)/shard_map/ppermute | solution.py:271
  283.3 3.0 %unpack.1 = f32[2,24,96,96]{3,2,1,0:T(8,128)} custom-call(s32[2]{0:T(128)S(1)} %pad_add_fusion.place, bf16[1728,128]{1,0:T(8,128)(2,1)S(1)} %collective-permute-done.11.refs_0_, bf16[1728,128]{1,0:T(8,128)(2,1)S(1)} %collective-permute-done.12.refs_1_, bf16[1728,128]{1,0:T(8,128)(2,1)S(1)} %collective-permute-done.13.refs_2_, ...), custom_call_target="tpu_custom_call" | custom-call | tf_op jit(solution)/shard_map/unpack/pallas_call | solution.py:131
  (82 shorter events, 13.7 us)
Async XLA Ops:
  0.0 17.1 %copy-start.25 = (f32[128]{0:T(128)S(1)}, f32[128]{0:T(128)}, u32[]{:S(2)}) copy-start(f32[128]{0:T(128)} %constant.66.clone) | copy-start | bytes 1540
  0.0 17.1 %copy-start.26 = (f32[96]{0:T(128)S(1)}, f32[96]{0:T(128)}, u32[]{:S(2)}) copy-start(f32[96]{0:T(128)} %constant.68.clone) | copy-start | bytes 1156
  3.1 50.9 %copy-start.1 = (bf16[1728,128]{1,0:T(8,128)(2,1)}, bf16[1728,128]{1,0:T(8,128)(2,1)S(1)}, u32[]{:S(2)}) copy-start(bf16[1728,128]{1,0:T(8,128)(2,1)S(1)} %get-tuple-element.33.refs_11_) | copy-start | bytes 1327108
  3.1 14.4 %collective-permute-start = (bf16[1728,128]{1,0:T(8,128)(2,1)S(1)}, bf16[1728,128]{1,0:T(8,128)(2,1)S(1)}, u32[]{:S(2)}, u32[]{:S(2)}) collective-permute-start(bf16[1728,128]{1,0:T(8,128)(2,1)S(1)} %get-tuple-element.31), channel_id=1, source_target_pairs={{0,252},{1,253},{2,254},{3,255},{4,0},{5,1},{6,2},{7,3},{8,4},{9,5... | collective-permute-start | bytes 1327112 | tf_op jit(solution)/shard_map/ppermute | solution.py:271
  5.0 31.5 %collective-permute-start.2 = (bf16[1728,128]{1,0:T(8,128)(2,1)S(1)}, bf16[1728,128]{1,0:T(8,128)(2,1)S(1)}, u32[]{:S(2)}, u32[]{:S(2)}) collective-permute-start(bf16[1728,128]{1,0:T(8,128)(2,1)S(1)} %get-tuple-element.31), channel_id=1, source_target_pairs={{0,254},{1,255},{2,252},{3,253},{4,2},{5,3},{6,0},{7,1},{8,6},{9,7... | collective-permute-start | bytes 1327112 | tf_op jit(solution)/shard_map/ppermute | solution.py:271
  14.1 20.1 %collective-permute-start.1 = (bf16[1728,128]{1,0:T(8,128)(2,1)S(1)}, bf16[1728,128]{1,0:T(8,128)(2,1)S(1)}, u32[]{:S(2)}, u32[]{:S(2)}) collective-permute-start(bf16[1728,128]{1,0:T(8,128)(2,1)S(1)} %get-tuple-element.32), channel_id=1, source_target_pairs={{0,253},{1,252},{2,255},{3,254},{4,1},{5,0},{6,3},{7,2},{8,5},{9,4... | collective-permute-start | bytes 1327112 | tf_op jit(solution)/shard_map/ppermute | solution.py:271
  14.1 29.8 %collective-permute-start.3 = (bf16[1728,128]{1,0:T(8,128)(2,1)S(1)}, bf16[1728,128]{1,0:T(8,128)(2,1)S(1)}, u32[]{:S(2)}, u32[]{:S(2)}) collective-permute-start(bf16[1728,128]{1,0:T(8,128)(2,1)S(1)} %get-tuple-element.32), channel_id=1, source_target_pairs={{0,255},{1,254},{2,253},{3,252},{4,3},{5,2},{6,1},{7,0},{8,7},{9,6... | collective-permute-start | bytes 1327112 | tf_op jit(solution)/shard_map/ppermute | solution.py:271
  16.0 71.3 %collective-permute-start.4 = (bf16[1728,128]{1,0:T(8,128)(2,1)S(1)}, bf16[1728,128]{1,0:T(8,128)(2,1)}, u32[]{:S(2)}, u32[]{:S(2)}) collective-permute-start(bf16[1728,128]{1,0:T(8,128)(2,1)S(1)} %get-tuple-element.34), channel_id=1, source_target_pairs={{0,1},{1,0},{2,3},{3,2},{4,5},{5,4},{6,7},{7,6},{8,9},{9,8},{10,11... | collective-permute-start | bytes 1327112 | tf_op jit(solution)/shard_map/ppermute | solution.py:271
  17.5 69.8 %copy-start.2 = (bf16[1728,128]{1,0:T(8,128)(2,1)}, bf16[1728,128]{1,0:T(8,128)(2,1)S(1)}, u32[]{:S(2)}) copy-start(bf16[1728,128]{1,0:T(8,128)(2,1)S(1)} %collective-permute-done.refs_7_) | copy-start | bytes 1327108
  17.5 69.7 %collective-permute-start.5 = (bf16[1728,128]{1,0:T(8,128)(2,1)S(1)}, bf16[1728,128]{1,0:T(8,128)(2,1)}, u32[]{:S(2)}, u32[]{:S(2)}) collective-permute-start(bf16[1728,128]{1,0:T(8,128)(2,1)S(1)} %get-tuple-element.34), channel_id=1, source_target_pairs={{0,2},{1,3},{2,0},{3,1},{4,6},{5,7},{6,4},{7,5},{8,10},{9,11},{10,... | collective-permute-start | bytes 1327112 | tf_op jit(solution)/shard_map/ppermute | solution.py:271
  34.2 53.1 %copy-start.6 = (bf16[1728,128]{1,0:T(8,128)(2,1)}, bf16[1728,128]{1,0:T(8,128)(2,1)S(1)}, u32[]{:S(2)}) copy-start(bf16[1728,128]{1,0:T(8,128)(2,1)S(1)} %collective-permute-done.1.refs_8_) | copy-start | bytes 1327108
  34.2 53.1 %collective-permute-start.6 = (bf16[1728,128]{1,0:T(8,128)(2,1)S(1)}, bf16[1728,128]{1,0:T(8,128)(2,1)}, u32[]{:S(2)}, u32[]{:S(2)}) collective-permute-start(bf16[1728,128]{1,0:T(8,128)(2,1)S(1)} %get-tuple-element.33.refs_11_), channel_id=1, source_target_pairs={{0,3},{1,2},{2,1},{3,0},{4,7},{5,6},{6,5},{7,4},{8,11},{9,10},{10,... | collective-permute-start | bytes 1327112 | tf_op jit(solution)/shard_map/ppermute | solution.py:271
  36.5 50.8 %copy-start.4 = (bf16[1728,128]{1,0:T(8,128)(2,1)}, bf16[1728,128]{1,0:T(8,128)(2,1)S(1)}, u32[]{:S(2)}) copy-start(bf16[1728,128]{1,0:T(8,128)(2,1)S(1)} %collective-permute-done.2.refs_9_) | copy-start | bytes 1327108
  36.5 42.3 %collective-permute-start.7 = (bf16[1728,128]{1,0:T(8,128)(2,1)S(1)}, bf16[1728,128]{1,0:T(8,128)(2,1)}, u32[]{:S(2)}, u32[]{:S(2)}) collective-permute-start(bf16[1728,128]{1,0:T(8,128)(2,1)S(1)} %get-tuple-element.35), channel_id=1, source_target_pairs={{0,8},{1,9},{2,10},{3,11},{4,12},{5,13},{6,14},{7,15},{8,16},{9,17... | collective-permute-start | bytes 1327112 | tf_op jit(solution)/shard_map/ppermute | solution.py:271
  43.9 43.4 %copy-start.8 = (bf16[1728,128]{1,0:T(8,128)(2,1)}, bf16[1728,128]{1,0:T(8,128)(2,1)S(1)}, u32[]{:S(2)}) copy-start(bf16[1728,128]{1,0:T(8,128)(2,1)S(1)} %collective-permute-done.3.refs_10_) | copy-start | bytes 1327108
  43.9 43.3 %collective-permute-start.9 = (bf16[1728,128]{1,0:T(8,128)(2,1)S(1)}, bf16[1728,128]{1,0:T(8,128)(2,1)}, u32[]{:S(2)}, u32[]{:S(2)}) collective-permute-start(bf16[1728,128]{1,0:T(8,128)(2,1)S(1)} %get-tuple-element.36), channel_id=1, source_target_pairs={{0,10},{1,11},{2,8},{3,9},{4,14},{5,15},{6,12},{7,13},{8,18},{9,19... | collective-permute-start | bytes 1327112 | tf_op jit(solution)/shard_map/ppermute | solution.py:271
  78.8 48.6 %collective-permute-start.8 = (bf16[1728,128]{1,0:T(8,128)(2,1)}, bf16[1728,128]{1,0:T(8,128)(2,1)S(1)}, u32[]{:S(2)}, u32[]{:S(2)}) collective-permute-start(bf16[1728,128]{1,0:T(8,128)(2,1)} %collective-permute-done.7.refs_15_), channel_id=1, source_target_pairs={{0,1},{1,0},{2,3},{3,2},{4,5},{5,4},{6,7},{7,6},{8,9},{9,8},{10,11... | collective-permute-start | bytes 1327112 | tf_op jit(solution)/shard_map/ppermute | solution.py:271
  87.2 40.2 %collective-permute-start.10 = (bf16[1728,128]{1,0:T(8,128)(2,1)}, bf16[1728,128]{1,0:T(8,128)(2,1)S(1)}, u32[]{:S(2)}, u32[]{:S(2)}) collective-permute-start(bf16[1728,128]{1,0:T(8,128)(2,1)} %collective-permute-done.9.refs_17_), channel_id=1, source_target_pairs={{0,1},{1,0},{2,3},{3,2},{4,5},{5,4},{6,7},{7,6},{8,9},{9,8},{10,11... | collective-permute-start | bytes 1327112 | tf_op jit(solution)/shard_map/ppermute | solution.py:271
  128.4 39.2 %copy-start.3 = (bf16[1728,128]{1,0:T(8,128)(2,1)S(1)}, bf16[1728,128]{1,0:T(8,128)(2,1)}, u32[]{:S(2)}) copy-start(bf16[1728,128]{1,0:T(8,128)(2,1)} %copy-done.2) | copy-start | bytes 1327108
  128.4 39.2 %copy-start.5 = (bf16[1728,128]{1,0:T(8,128)(2,1)S(1)}, bf16[1728,128]{1,0:T(8,128)(2,1)}, u32[]{:S(2)}) copy-start(bf16[1728,128]{1,0:T(8,128)(2,1)} %copy-done.4) | copy-start | bytes 1327108
  128.4 39.2 %copy-start.7 = (bf16[1728,128]{1,0:T(8,128)(2,1)S(1)}, bf16[1728,128]{1,0:T(8,128)(2,1)}, u32[]{:S(2)}) copy-start(bf16[1728,128]{1,0:T(8,128)(2,1)} %copy-done.6) | copy-start | bytes 1327108
  128.4 39.2 %copy-start.9 = (bf16[1728,128]{1,0:T(8,128)(2,1)S(1)}, bf16[1728,128]{1,0:T(8,128)(2,1)}, u32[]{:S(2)}) copy-start(bf16[1728,128]{1,0:T(8,128)(2,1)} %copy-done.8) | copy-start | bytes 1327108
  204.0 2.7 collective-permute-start.18
  204.5 16.1 %collective-permute-start.11 = (bf16[1728,128]{1,0:T(8,128)(2,1)}, bf16[1728,128]{1,0:T(8,128)(2,1)S(1)}, u32[]{:S(2)}, u32[]{:S(2)}) collective-permute-start(bf16[1728,128]{1,0:T(8,128)(2,1)} %get-tuple-element.41), channel_id=1, source_target_pairs={{0,4},{1,5},{2,6},{3,7},{4,8},{5,9},{6,10},{7,11},{8,12},{9,13},{1... | collective-permute-start | bytes 1327112 | tf_op jit(solution)/shard_map/ppermute | solution.py:271
  204.5 24.4 %collective-permute-start.12 = (bf16[1728,128]{1,0:T(8,128)(2,1)}, bf16[1728,128]{1,0:T(8,128)(2,1)S(1)}, u32[]{:S(2)}, u32[]{:S(2)}) collective-permute-start(bf16[1728,128]{1,0:T(8,128)(2,1)} %get-tuple-element.42), channel_id=1, source_target_pairs={{0,5},{1,4},{2,7},{3,6},{4,9},{5,8},{6,11},{7,10},{8,13},{9,12},{1... | collective-permute-start | bytes 1327112 | tf_op jit(solution)/shard_map/ppermute | solution.py:271
  204.5 34.1 %collective-permute-start.13 = (bf16[1728,128]{1,0:T(8,128)(2,1)}, bf16[1728,128]{1,0:T(8,128)(2,1)S(1)}, u32[]{:S(2)}, u32[]{:S(2)}) collective-permute-start(bf16[1728,128]{1,0:T(8,128)(2,1)} %get-tuple-element.43), channel_id=1, source_target_pairs={{0,6},{1,7},{2,4},{3,5},{4,10},{5,11},{6,8},{7,9},{8,14},{9,15},{1... | collective-permute-start | bytes 1327112 | tf_op jit(solution)/shard_map/ppermute | solution.py:271
  204.5 42.5 %collective-permute-start.14 = (bf16[1728,128]{1,0:T(8,128)(2,1)}, bf16[1728,128]{1,0:T(8,128)(2,1)S(1)}, u32[]{:S(2)}, u32[]{:S(2)}) collective-permute-start(bf16[1728,128]{1,0:T(8,128)(2,1)} %get-tuple-element.44), channel_id=1, source_target_pairs={{0,7},{1,6},{2,5},{3,4},{4,11},{5,10},{6,9},{7,8},{8,15},{9,14},{1... | collective-permute-start | bytes 1327112 | tf_op jit(solution)/shard_map/ppermute | solution.py:271
  207.7 47.3 %collective-permute-start.15 = (bf16[1728,128]{1,0:T(8,128)(2,1)}, bf16[1728,128]{1,0:T(8,128)(2,1)S(1)}, u32[]{:S(2)}, u32[]{:S(2)}) collective-permute-start(bf16[1728,128]{1,0:T(8,128)(2,1)} %get-tuple-element.50), channel_id=1, source_target_pairs={{0,1},{1,0},{2,3},{3,2},{4,5},{5,4},{6,7},{7,6},{8,9},{9,8},{10,11... | collective-permute-start | bytes 1327112 | tf_op jit(solution)/shard_map/ppermute | solution.py:271
  220.6 34.4 %collective-permute-start.16 = (bf16[1728,128]{1,0:T(8,128)(2,1)S(1)}, bf16[1728,128]{1,0:T(8,128)(2,1)S(1)}, u32[]{:S(2)}, u32[]{:S(2)}) collective-permute-start(bf16[1728,128]{1,0:T(8,128)(2,1)S(1)} %get-tuple-element.51), channel_id=1, source_target_pairs={{0,2},{1,3},{2,0},{3,1},{4,6},{5,7},{6,4},{7,5},{8,10},{9,11},{10,... | collective-permute-start | bytes 1327112 | tf_op jit(solution)/shard_map/ppermute | solution.py:271
  229.0 35.1 %collective-permute-start.17 = (bf16[1728,128]{1,0:T(8,128)(2,1)S(1)}, bf16[1728,128]{1,0:T(8,128)(2,1)S(1)}, u32[]{:S(2)}, u32[]{:S(2)}) collective-permute-start(bf16[1728,128]{1,0:T(8,128)(2,1)S(1)} %get-tuple-element.52), channel_id=1, source_target_pairs={{0,3},{1,2},{2,1},{3,0},{4,7},{5,6},{6,5},{7,4},{8,11},{9,10},{10,... | collective-permute-start | bytes 1327112 | tf_op jit(solution)/shard_map/ppermute | solution.py:271
  238.6 37.7 %collective-permute-start.19 = (bf16[1728,128]{1,0:T(8,128)(2,1)}, bf16[1728,128]{1,0:T(8,128)(2,1)S(1)}, u32[]{:S(2)}, u32[]{:S(2)}) collective-permute-start(bf16[1728,128]{1,0:T(8,128)(2,1)} %get-tuple-element.55), channel_id=1, source_target_pairs={{0,248},{1,249},{2,250},{3,251},{4,252},{5,253},{6,254},{7,255},{8... | collective-permute-start | bytes 1327112 | tf_op jit(solution)/shard_map/ppermute | solution.py:271
  247.1 36.2 %collective-permute-start.20 = (bf16[1728,128]{1,0:T(8,128)(2,1)}, bf16[1728,128]{1,0:T(8,128)(2,1)S(1)}, u32[]{:S(2)}, u32[]{:S(2)}) collective-permute-start(bf16[1728,128]{1,0:T(8,128)(2,1)} %get-tuple-element.56), channel_id=1, source_target_pairs={{0,250},{1,251},{2,248},{3,249},{4,254},{5,255},{6,252},{7,253},{8... | collective-permute-start | bytes 1327112 | tf_op jit(solution)/shard_map/ppermute | solution.py:271
  (18 other events, 46.4 us)
